TPU v7x, 32 devices: a whole 2x2x4 slice. The times are simulated.
32 devices in a mesh: groups: 2 (over y), space: 8 (over z, core), tm: 2 (over x), rep: 1.
Axes of the slice: x: 2, y: 2, z: 4, core: 2. Of those that a mesh axis runs over, the one named last changes fastest.
Arguments:
- noise: float32 [8192, 4096], P(('groups', 'space'), 'tm'), parts along dimension 0, may hold values from -6 to 6
- factor: float32 [4096, 4096], P(('tm', 'rep'), 'space'), may hold values from -8 to 8, as said below
- col_blocks: int32 [64, 4], P(('groups', 'space')), parts along dimension 0, may hold values from 0 to 31, as said below
- block_values: float32 [64, 4, 128, 128], P(('groups', 'space')), parts along dimension 0, may hold values from -0.25 to 0.25
Outputs:
- samples: float32 [8192, 4096], P(('groups', 'space'), ('tm', 'rep')), parts along dimension 0
There are 2 independent parts, one for each index of `groups`. A program takes and returns all parts, laid end to end along the dimension named above; an argument that names none is the same for every part. Nothing has to cross between parts.
Inputs may be any that keep to these rules, and one draw needn't show every extreme that they name: factor is lower triangular: every entry above the diagonal is zero, and the diagonal lies in 0.5 to 1.5. `col_blocks`: in every row b the first entry is b itself; the other 3 entries are distinct blocks whose circular distance from b (modulo 32) is 1 to 2.
All inputs are finite; a program needn't handle non-finite values.
Results may differ from a plain program's by a relative error of at most 0.0003.
Values sent between devices are 32-bit elements; how exact they have to be, the bound alone decides.
A program may use at most 128 MiB of HBM per device.

v0:
```python
import jax
import jax.numpy as jnp
from jax import lax
from jax.sharding import PartitionSpec as P

BS = 128
REACH = 2


def shifted(block, axis, distance):
    devices = range(lax.axis_size(axis))
    route = [(i - distance, i) for i in devices if i - distance in devices]
    return lax.ppermute(block, axis, route)


def extended_2(block, sides, width):
    for axis, dim in sides:
        count = lax.axis_size(axis)
        forward = [(i, i + 1) for i in range(count - 1)]
        forward.append((count - 1, 0))
        backward = [(target, source) for source, target in forward]
        low = lax.ppermute(
            lax.slice_in_dim(block, block.shape[dim] - width, None, axis=dim), axis, forward
        )
        high = lax.ppermute(lax.slice_in_dim(block, 0, width, axis=dim), axis, backward)
        block = jnp.concatenate([low, block, high], axis=dim)
    return block


def per_device(noise, factor, col_blocks, block_values):
    node_rows = noise.shape[0]
    hour_cols = noise.shape[1]
    tm_index = lax.axis_index("tm")
    tm_count = lax.axis_size("tm")
    every_hour = jnp.zeros((node_rows, hour_cols * tm_count), jnp.float32)
    every_hour = lax.dynamic_update_slice_in_dim(every_hour, noise, tm_index * hour_cols, 1)
    moving = noise
    for step in range(1, tm_count):
        moving = shifted(moving, "tm", 1)
        slot = jnp.maximum(tm_index - step, 0) * hour_cols
        placed = lax.dynamic_update_slice_in_dim(every_hour, moving, slot, 1)
        every_hour = jnp.where(tm_index >= step, placed, every_hour)
    colored = lax.dot_general(
        every_hour,
        lax.all_gather(factor, "space", axis=1, tiled=True),
        (((1,), (1,)), ((), ())),
        precision=lax.Precision.HIGHEST,
        preferred_element_type=jnp.float32,
    )
    extended = extended_2(colored, (("space", 0),), REACH * BS)
    local_blocks = node_rows // BS
    out_cols = colored.shape[1]
    ext_blocks = extended.reshape(local_blocks + 2 * REACH, BS, out_cols)
    all_blocks = lax.axis_size("space") * local_blocks
    local_rows = jnp.arange(local_blocks, dtype=jnp.int32)[:, None]
    global_rows = lax.axis_index("space") * local_blocks + local_rows
    offsets = (col_blocks - global_rows + REACH) % all_blocks - REACH
    positions = local_rows + REACH + offsets
    picked = ext_blocks[positions]
    result = jnp.einsum("nkab,nkbh->nah", block_values, picked, precision=lax.Precision.HIGHEST)
    return result.reshape(node_rows, out_cols)


def solution(mesh):
    return jax.shard_map(
        per_device,
        mesh=mesh,
        in_specs=(
            P(("groups", "space"), "tm"),
            P(("tm", "rep"), "space"),
            P(("groups", "space"), None),
            P(("groups", "space"), None, None, None),
        ),
        out_specs=P(("groups", "space"), ("tm", "rep")),
        check_vma=False,
    )
```

profile of v0, /device:TPU:3, one launch (start us, length us, event | category | flops | bytes accessed | tf_op | source)
XLA Modules:
  0.0 446.7 jit_solution(9895273938419054406)
XLA Ops:
  6.5 0.0 copy-start
  6.5 0.0 all-gather.2.cloned.1.call-start
  6.5 0.7 all-gather.2.cloned.1.call-update
  7.3 1.3 collective-permute-start
  8.6 0.0 copy-start.2
  8.6 4.2 broadcast_in_dim.7
  12.8 0.0 copy-done.2
  12.8 2.2 constant_dynamic-update-slice_fusion
  15.1 85.8 %collective-permute-done = f32[512,2048]{1,0:T(8,128)} collective-permute-done((f32[512,2048]{1,0:T(8,128)}, f32[512,2048]{1,0:T(8,128)}, u32[]{:S(2)}, u32[]{:S(2)}) %collective-permute-start) | collective-permute-done | bytes 4194336 | tf_op jit(solution)/shard_map/ppermute | solution.py:13
  100.9 6.5 %select_dynamic-update-slice_fusion = f32[512,4096]{1,0:T(8,128)} fusion(f32[512,4096]{1,0:T(8,128)} %constant_dynamic-update-slice_fusion, s32[]{:T(128)S(6)} %select_n.30, f32[512,2048]{1,0:T(8,128)} %collective-permute-done, pred[]{:T(512)S(6)} %ge.3), kind=kLoop, calls=%fused_computation.2 | loop fusion | flops 1048576 | bytes 12582917 | tf_op jit(solution)/shard_map/jit(_where)/select_n | solution.py:42
  107.4 191.9 %all-gather.2.cloned.1.call-done = f32[2048,4096]{1,0:T(8,128)} async-done(((f32[2048,512]{1,0:T(8,128)}), f32[2048,4096]{1,0:T(8,128)}) %all-gather.2.cloned.1.call-update) | async-done | bytes 33554448 | tf_op jit(solution)/shard_map/all_gather | solution.py:45
  299.3 59.7 %fusion.4 = f32[512,2048]{1,0:T(8,128)S(1)} fusion(f32[512,4096]{1,0:T(8,128)} %select_dynamic-update-slice_fusion, f32[2048,4096]{1,0:T(8,128)} %all-gather.2.cloned.1.call-done), kind=kOutput, calls=%fused_computation.15 | convolution fusion | flops 51539607552 | bytes 46137344 | tf_op jit(solution)/shard_map/dot_general | solution.py:43
  359.0 0.0 copy-start.1
  359.0 2.0 copy-done.1
  361.0 0.0 copy-start.3
  361.0 1.6 fusion.3
  362.6 0.0 collective-permute-start.1
  362.6 0.5 collective-permute-start.2
  363.1 0.0 copy-done.3
  363.1 0.1 compare_select_fusion
  363.2 0.1 reshape.20
  363.3 41.2 %collective-permute-done.1 = f32[256,2048]{1,0:T(8,128)} collective-permute-done((f32[256,2048]{1,0:T(8,128)}, f32[256,2048]{1,0:T(8,128)}, u32[]{:S(2)}, u32[]{:S(2)}) %collective-permute-start.1) | collective-permute-done | bytes 2097184 | tf_op jit(solution)/shard_map/ppermute | solution.py:22
  404.6 4.8 %collective-permute-done.2 = f32[256,2048]{1,0:T(8,128)} collective-permute-done((f32[256,2048]{1,0:T(8,128)S(1)}, f32[256,2048]{1,0:T(8,128)}, u32[]{:S(2)}, u32[]{:S(2)}) %collective-permute-start.2) | collective-permute-done | bytes 2097184 | tf_op jit(solution)/shard_map/ppermute | solution.py:25
  409.4 6.0 %pad_maximum_fusion = f32[1024,2048]{1,0:T(8,128)} fusion(f32[256,2048]{1,0:T(8,128)} %collective-permute-done.2, f32[512,2048]{1,0:T(8,128)} %copy-done.1, f32[256,2048]{1,0:T(8,128)} %collective-permute-done.1), kind=kLoop, calls=%fused_computation.1 | loop fusion | flops 4194304 | bytes 16777216 | tf_op jit(solution)/shard_map/concatenate | solution.py:26
  415.3 11.5 %gather_fusion = f32[16,128,2048]{2,1,0:T(8,128)} fusion(f32[8,128,2048]{2,1,0:T(8,128)} %bitcast.12, s32[1024]{0:T(1024)S(1)} %pad_clamp_fusion), kind=kCustom, calls=%fused_computation | custom fusion | bytes 33554496 | tf_op jit(solution)/shard_map/gather | solution.py:59
  426.8 0.0 copy-done
  426.8 13.1 %fusion.5 = f32[4,2048,128,1]{1,2,3,0:T(8,128)} fusion(f32[4,4,128,2048]{3,2,1,0:T(8,128)} %bitcast.13, f32[4,4,128,128]{3,2,1,0:T(8,128)S(1)} %copy-done), kind=kOutput, calls=%fused_computation.16 | convolution fusion | flops 6442450944 | bytes 22020096 | tf_op jit(solution)/shard_map/nkab,nkbh->nah/dot_general | solution.py:60
  (2 shorter events, 0.0 us)
Async XLA Ops:
  6.5 420.3 %copy-start = (f32[4,4,128,128]{3,2,1,0:T(8,128)S(1)}, f32[4,4,128,128]{3,2,1,0:T(8,128)}, u32[]{:S(2)}) copy-start(f32[4,4,128,128]{3,2,1,0:T(8,128)} %param.7) | copy-start | bytes 3145732
  6.5 292.7 %all-gather.2.cloned.1.call-start = ((), (), s32[]{:S(2)}) async-start(), calls=%async_computation | async-start | bytes 37748736 | tf_op jit(solution)/shard_map/all_gather | solution.py:45
  7.3 93.7 %collective-permute-start = (f32[512,2048]{1,0:T(8,128)}, f32[512,2048]{1,0:T(8,128)}, u32[]{:S(2)}, u32[]{:S(2)}) collective-permute-start(f32[512,2048]{1,0:T(8,128)} %param.4), channel_id=1, source_target_pairs={{0,1},{2,3},{4,5},{6,7},{8,9},{10,11},{12,13},{14,15},{16,17},{18,... | collective-permute-start | bytes 12582920 | tf_op jit(solution)/shard_map/ppermute | solution.py:13
  8.6 4.3 copy-start.2
  359.0 2.0 copy-start.1
  361.0 2.1 copy-start.3
  362.6 41.9 %collective-permute-start.1 = (f32[256,2048]{1,0:T(8,128)}, f32[256,2048]{1,0:T(8,128)}, u32[]{:S(2)}, u32[]{:S(2)}) collective-permute-start(f32[256,2048]{1,0:T(8,128)} %get-tuple-element.5), channel_id=1, source_target_pairs={{0,2},{2,4},{4,6},{6,8},{8,10},{10,12},{12,14},{14,0},{1,3},{3,5},... | collective-permute-start | bytes 6291464 | tf_op jit(solution)/shard_map/ppermute | solution.py:22
  362.6 46.7 %collective-permute-start.2 = (f32[256,2048]{1,0:T(8,128)S(1)}, f32[256,2048]{1,0:T(8,128)}, u32[]{:S(2)}, u32[]{:S(2)}) collective-permute-start(f32[256,2048]{1,0:T(8,128)S(1)} %get-tuple-element.6), channel_id=1, source_target_pairs={{2,0},{4,2},{6,4},{8,6},{10,8},{12,10},{14,12},{0,14},{3,1},{5,3},... | collective-permute-start | bytes 6291464 | tf_op jit(solution)/shard_map/ppermute | solution.py:25
Sparse Core Ops, SparseCore 0:
  9.0 290.2 all-gather.1
where the time goes:
time: 450 us; the launch traced here: 447 us
  waiting for transfers between devices  324 us (72%)
  matrix products  72.8 us (16%)
  local copies, waits for them, and re-layouts  21.7 us (5%)
  between operations  13.4 us (3%)
  other arithmetic  12.6 us (3%)
    all_gather x1, waiting for transfers between devices, per_device(): lax.all_gather(factor, 'space', axis=1, tiled=True)  192 us
    ppermute x1, waiting for transfers between devices, shifted(): return lax.ppermute(block, axis, route)  85.8 us
    dot_general x1, matrix products, per_device(): lax.dot_general(every_hour, lax.all_gather(factor, 'space', axis=1, tiled...  59.7 us
    ppermute x1, waiting for transfers between devices, extended_2(): lax.ppermute(lax.slice_in_dim(block, block.shape[dim] - width, None, axis...  41.2 us
    dot_general x1, matrix products, per_device(): jnp.einsum('nkab,nkbh->nah', block_values, picked, precision=lax.Precisio...  13.1 us
    gather x1, local copies, waits for them, and re-layouts, per_device(): picked = ext_blocks[positions]  11.5 us
  transfers between devices with their start and end apart: 4, of which 4 were waited for; matrix products, arithmetic and copies ran while one was open for 3% of the time, Pallas kernels for 0%

commit v1 on v0

--- a/solution.py
+++ b/solution.py
@@ -1,6 +1,10 @@
+import functools
+
 import jax
 import jax.numpy as jnp
 from jax import lax
+from jax.experimental import pallas as pl
+from jax.experimental.pallas import tpu as pltpu
 from jax.sharding import PartitionSpec as P
 
 BS = 128
@@ -61,9 +65,274 @@
     return result.reshape(node_rows, out_cols)
 
 
+MESH = pl.DeviceIdType.MESH
+
+
+def split(x):
+    high = x.astype(jnp.bfloat16)
+    return high, (x - high.astype(jnp.float32)).astype(jnp.bfloat16)
+
+
+def dot3(a, b, dims):
+    (ah, al), (bh, bl) = a, b
+    dot = functools.partial(
+        lax.dot_general, dimension_numbers=dims, preferred_element_type=jnp.float32
+    )
+    return dot(ah, bh) + (dot(ah, bl) + dot(al, bh))
+
+
+def fused_kernel(
+    count, noise, factor, cols, values, out,
+    fac, ext, qn, wh, wl,
+    s_chain, r_chain, s_other, r_other, s_halo, r_halo, s_qn, r_qn, s_loc, s_own,
+):
+    d, m, y = lax.axis_index("space"), lax.axis_index("tm"), lax.axis_index("groups")
+    core = lax.rem(d, 2)
+    width = factor.shape[1]
+    half = width // 2
+    hb = factor.shape[0] // width
+    steps = count * hb
+    rows = noise.shape[0]
+    reach = REACH * BS
+    local = rows // BS
+
+    def at(**where):
+        return {k: v for k, v in where.items()}
+
+    right, left = lax.rem(d + 1, count), lax.rem(d + count - 1, count)
+    sibling = d + 1 - 2 * core
+    barrier = pltpu.get_barrier_semaphore()
+    for where in (at(space=right), at(space=left), at(tm=1 - m), at(groups=1 - y)):
+        pl.semaphore_signal(barrier, inc=1, device_id=where, device_id_type=MESH)
+
+    def slot(i, j):
+        a = i - hb
+        return jnp.where(i < hb, i * hb + j, hb * hb + hb * a - a * (a - 1) // 2 + j - a)
+
+    def valid(i, j):
+        return (i >= 0) & (i < count) & (j >= i - hb * m)
+
+    def rows_of(i, j, h):
+        return fac.at[slot(i, j), pl.ds(pl.multiple_of(h * half, half), half), :]
+
+    def chain(i, j, way):
+        to = jnp.where(way == 0, right, left)
+        return pltpu.make_async_remote_copy(
+            src_ref=rows_of(i, j, y), dst_ref=rows_of(i, j, y),
+            send_sem=s_chain.at[way, slot(i, j)], recv_sem=r_chain.at[slot(i, j)],
+            device_id=at(space=to), device_id_type=MESH,
+        )
+
+    def cross(i, j):
+        return pltpu.make_async_remote_copy(
+            src_ref=rows_of(i, j, y), dst_ref=rows_of(i, j, y),
+            send_sem=s_other.at[slot(i, j)], recv_sem=r_other.at[slot(i, j)],
+            device_id=at(groups=1 - y), device_id_type=MESH,
+        )
+
+    def share(i, j):
+        return pltpu.make_async_remote_copy(
+            src_ref=rows_of(i, j, 1 - y), dst_ref=rows_of(i, j, 1 - y),
+            send_sem=s_own.at[slot(i, j)], recv_sem=r_other.at[slot(i, j)],
+            device_id=at(space=sibling), device_id_type=MESH,
+        )
+
+    def halo(c, way):
+        if way == 0:
+            src, dst, to = rows - reach, 0, right
+        else:
+            src, dst, to = 0, reach + rows, left
+        return pltpu.make_async_remote_copy(
+            src_ref=noise.at[pl.ds(src, reach), pl.ds(pl.multiple_of(c * width, width), width)],
+            dst_ref=ext.at[c, pl.ds(dst, reach), :],
+            send_sem=s_halo.at[way, c], recv_sem=r_halo.at[way, c],
+            device_id=at(space=to), device_id_type=MESH,
+        )
+
+    def centre(c):
+        return pltpu.make_async_copy(
+            noise.at[:, pl.ds(c * width, width)], ext.at[c, pl.ds(reach, rows), :], s_loc.at[0, c]
+        )
+
+    def own_factor(j):
+        return pltpu.make_async_copy(
+            factor.at[pl.ds(j * width, width), :], fac.at[slot(d, j)], s_loc.at[1, j]
+        )
+
+    def give(c):
+        return pltpu.make_async_remote_copy(
+            src_ref=qn.at[c], dst_ref=qn.at[c], send_sem=s_qn.at[c], recv_sem=r_qn.at[c],
+            device_id=at(tm=1 - m), device_id_type=MESH,
+        )
+
+    for j in range(hb):
+        centre(j).start()
+        pl.when(valid(d, j))(lambda j=j: own_factor(j).start())
+    pl.semaphore_wait(barrier, 4)
+    for c in reversed(range(hb)):
+        halo(c, 0).start()
+        halo(c, 1).start()
+
+    for j in range(hb):
+        @pl.when(valid(d, j))
+        def _(j=j):
+            own_factor(j).wait()
+            pl.when(d < count - 1)(lambda: chain(d, j, 0).start())
+            pl.when(d > 0)(lambda: chain(d, j, 1).start())
+            share(d, j).start()
+
+    out[...] = jnp.zeros_like(out)
+    wh[...] = jnp.zeros_like(wh)
+    wl[...] = jnp.zeros_like(wl)
+    blocks = count * local
+    for b in range(local):
+        place = [
+            lax.rem(cols[b, k] - (d * local + b) + REACH + blocks, blocks)
+            for k in range(values.shape[1])
+        ]
+        for o in range(2 * REACH + 1):
+            total = jnp.zeros((BS, BS), jnp.float32)
+            for k, where in enumerate(place):
+                total = total + values[b, k] * (where == o).astype(jnp.float32)
+            high, low = split(total)
+            wh[b * BS:(b + 1) * BS, (b + o) * BS:(b + o + 1) * BS] = high
+            wl[b * BS:(b + 1) * BS, (b + o) * BS:(b + o + 1) * BS] = low
+    for c in range(hb):
+        centre(c).wait()
+
+    def source(a, way):
+        return jnp.where(way == 0, d - 1 - a, d + 1 + a)
+
+    def apart(i):
+        return i // 2 != d // 2
+
+    def body(n, carry):
+        a, j = n // hb, lax.rem(n, hb)
+        for way in (0, 1):
+            i = source(a, way)
+
+            @pl.when(valid(i, j))
+            def _(i=i, way=way):
+                chain(i, j, way).wait_recv()
+                more = (d < count - 1) if way == 0 else (d > 0)
+                pl.when(more)(lambda: chain(i, j, way).start())
+                pl.when(apart(i) & (lax.rem(j, 2) == core))(lambda: cross(i, j).start())
+
+        before = jnp.maximum(n - 1, 0)
+        b, k = before // hb, lax.rem(before, hb)
+        for way in (0, 1):
+            i = source(b, way)
+
+            @pl.when((n > 0) & valid(i, k) & apart(i) & (lax.rem(k, 2) == core))
+            def _(i=i):
+                cross(i, k).wait_recv()
+                share(i, k).start()
+
+        @pl.when(n < hb)
+        def _():
+            c = hb - 1 - n
+            halo(c, 0).wait_recv()
+            halo(c, 1).wait_recv()
+            q = dot3((wh[...], wl[...]), split(ext[c]), (((1,), (0,)), ((), ())))
+            qn[m * hb + c] = q
+            pl.when(m == 0)(lambda: give(c).start())
+
+        for way in (0, 1):
+            i = source(a - 1, way)
+
+            @pl.when((a > 0) & valid(i, j) & ((lax.rem(j, 2) != core) | (i // 2 == d // 2)))
+            def _(i=i):
+                share(i, j).wait_recv()
+
+        early = 2 * hb - a - 1 + 0 * j
+        pl.when((j == 0) & (m == 1) & (a >= count - hb) & (a < count))(
+            lambda: give(early).wait_recv()
+        )
+
+        def product(which, carry):
+            i = jnp.where(
+                which == 0, d - a, jnp.where(which == 1, d + a, jnp.where(which == 2, d, early))
+            )
+            late = (i >= hb) & (a > 0) & ((which != 2) | (a == 1))
+            fits = jnp.where(which == 3, a >= count - hb, late)
+
+            @pl.when(fits & valid(i, j))
+            def _():
+                at_cols = pl.ds(pl.multiple_of(j * width, width), width)
+                out[:, at_cols] += dot3(
+                    split(qn[i]), split(fac[slot(i, j)]), (((1,), (1,)), ((), ()))
+                )
+
+            return carry
+
+        return lax.fori_loop(0, 4, product, carry)
+
+    lax.fori_loop(0, steps, body, 0)
+
+    for c in range(hb):
+        halo(c, 0).wait_send()
+        halo(c, 1).wait_send()
+        pl.when(m == 0)(lambda c=c: give(c).wait_send())
+
+    def drain(n, carry):
+        i, j = n // hb, lax.rem(n, hb)
+
+        @pl.when(valid(i, j))
+        def _():
+            pl.when((i <= d) & (d < count - 1))(lambda: chain(i, j, 0).wait_send())
+            pl.when((i >= d) & (d > 0))(lambda: chain(i, j, 1).wait_send())
+            mine = apart(i) & (lax.rem(j, 2) == core)
+            pl.when(mine)(lambda: cross(i, j).wait_send())
+            pl.when(mine | (i == d))(lambda: share(i, j).wait_send())
+
+        return carry
+
+    lax.fori_loop(0, steps, drain, 0)
+
+
+def fused(noise, factor, col_blocks, block_values):
+    count = lax.axis_size("space")
+    rows, width = noise.shape[0], factor.shape[1]
+    hb = factor.shape[0] // width
+    slots = hb * hb + hb * (hb + 1) // 2
+    dma = pltpu.SemaphoreType.DMA
+    return pl.pallas_call(
+        functools.partial(fused_kernel, count),
+        out_shape=jax.ShapeDtypeStruct(noise.shape, jnp.float32),
+        in_specs=[
+            pl.BlockSpec(memory_space=pl.ANY),
+            pl.BlockSpec(memory_space=pl.ANY),
+            pl.BlockSpec(memory_space=pltpu.SMEM),
+            pl.BlockSpec(memory_space=pltpu.VMEM),
+        ],
+        out_specs=pl.BlockSpec(memory_space=pltpu.VMEM),
+        scratch_shapes=[
+            pltpu.VMEM((slots, width, width), jnp.float32),
+            pltpu.VMEM((hb, rows + 2 * REACH * BS, width), jnp.float32),
+            pltpu.VMEM((2 * hb, rows, width), jnp.float32),
+            pltpu.VMEM((rows, rows + 2 * REACH * BS), jnp.bfloat16),
+            pltpu.VMEM((rows, rows + 2 * REACH * BS), jnp.bfloat16),
+            dma((2, slots)), dma((slots,)), dma((slots,)), dma((slots,)),
+            dma((2, hb)), dma((2, hb)), dma((2 * hb,)), dma((2 * hb,)),
+            dma((2, hb)), dma((slots,)),
+        ],
+        compiler_params=pltpu.CompilerParams(
+            collective_id=0, has_side_effects=True, vmem_limit_bytes=62 * 1024 * 1024
+        ),
+    )(noise, factor, col_blocks, block_values)
+
+
+def fits_fused(mesh):
+    shape = mesh.shape
+    return (
+        shape["tm"] == 2 and shape["rep"] == 1 and shape["groups"] == 2
+        and shape["space"] % 2 == 0 and shape["space"] >= 4
+    )
+
+
 def solution(mesh):
     return jax.shard_map(
-        per_device,
+        fused if fits_fused(mesh) else per_device,
         mesh=mesh,
         in_specs=(
             P(("groups", "space"), "tm"),

time: 450 us -> 225 us (0.50)
  waiting for transfers between devices: 324 us -> 0 us
  Pallas kernels: 0 us -> 220 us
  matrix products: 72.8 us -> 0 us
  local copies, waits for them, and re-layouts: 21.7 us -> 4.7 us
  between operations: 13.4 us -> 0.01 us
  other arithmetic: 12.6 us -> 0 us
    pallas_call x0 -> x1, Pallas kernels: none -> 220 us  [fused(): pl.pallas_call(functools.partial(fused_kernel, count), out_shape=jax.Shap...]
    all_gather x1 -> x0, waiting for transfers between devices: 192 us -> none  [per_device(): lax.all_gather(factor, 'space', axis=1, tiled=True)]
    ppermute x3 -> x0, waiting for transfers between devices: 132 us -> none  [the longest x1 85.8 us: shifted(): return lax.ppermute(block, axis, route)]
    dot_general x2 -> x0, matrix products: 72.8 us -> none  [the longest x1 59.7 us: per_device(): lax.dot_general(every_hour, lax.all_gather(factor, 'space', axis=1, tiled...]
    gather x1 -> x0, local copies, waits for them, and re-layouts: 11.5 us -> none  [per_device(): picked = ext_blocks[positions]]
    select_n x2 -> x0, other arithmetic: 6.58 us -> none  [the longest x1 6.49 us: per_device(): every_hour = jnp.where(tm_index >= step, placed, every_hour)]
    concatenate x1 -> x0, other arithmetic: 5.98 us -> none  [extended_2(): block = jnp.concatenate([low, block, high], axis=dim)]
  transfers between devices with their start and end apart: 4 -> 0, of which waited for: 4 -> 0; matrix products, arithmetic and copies ran while one was open for 3% -> 0% of each run, Pallas kernels for 0% -> 0%
where the time goes in v1:
time: 225 us
  Pallas kernels  220 us (98%)
  local copies, waits for them, and re-layouts  4.7 us (2%)
    pallas_call x1, Pallas kernels, fused(): pl.pallas_call(functools.partial(fused_kernel, count), out_shape=jax.Shap...  220 us
    unnamed x1, local copies, waits for them, and re-layouts  4.7 us

profile of v1, /device:TPU:3, one launch (start us, length us, event | category | flops | bytes accessed | tf_op | source)
XLA Modules:
  0.0 224.5 jit_solution(6957479902443658611)
XLA Ops:
  0.0 219.8 %shard_map.46 = f32[512,2048]{1,0:T(8,128)} custom-call(f32[512,2048]{1,0:T(8,128)} %noise.1, f32[2048,512]{1,0:T(8,128)} %factor.1, s32[4,4]{1,0:T(4,128)} %cols.1, f32[4,4,128,128]{3,2,1,0:T(8,128)} %values.1), custom_call_target="tpu_custom_call" | custom-call | tf_op jit(solution)/shard_map/pallas_call | solution.py:299
  219.8 4.7 %copy.6 = f32[512,2048]{1,0:T(8,128)} copy(f32[512,2048]{1,0:T(8,128)} %shard_map.46) | data formatting | bytes 8388608

commit v2 on v1

--- a/solution.py
+++ b/solution.py
@@ -169,11 +169,10 @@
         centre(j).start()
         pl.when(valid(d, j))(lambda j=j: own_factor(j).start())
     pl.semaphore_wait(barrier, 4)
-    for c in reversed(range(hb)):
-        halo(c, 0).start()
-        halo(c, 1).start()
-
     for j in range(hb):
+        halo(hb - 1 - j, 0).start()
+        halo(hb - 1 - j, 1).start()
+
         @pl.when(valid(d, j))
         def _(j=j):
             own_factor(j).wait()
@@ -228,9 +227,9 @@
                 cross(i, k).wait_recv()
                 share(i, k).start()
 
-        @pl.when(n < hb)
+        @pl.when((lax.rem(n, hb - 1) == 0) & (n > 0) & (n <= hb * (hb - 1)))
         def _():
-            c = hb - 1 - n
+            c = hb - n // (hb - 1)
             halo(c, 0).wait_recv()
             halo(c, 1).wait_recv()
             q = dot3((wh[...], wl[...]), split(ext[c]), (((1,), (0,)), ((), ())))
@@ -250,11 +249,9 @@
         )
 
         def product(which, carry):
-            i = jnp.where(
-                which == 0, d - a, jnp.where(which == 1, d + a, jnp.where(which == 2, d, early))
-            )
-            late = (i >= hb) & (a > 0) & ((which != 2) | (a == 1))
-            fits = jnp.where(which == 3, a >= count - hb, late)
+            i = jnp.where(which == hb, early, hb + which)
+            away = jnp.maximum(jnp.maximum(d - i, i - d), count - hb)
+            fits = jnp.where(which == hb, a >= count - hb, a == away)
 
             @pl.when(fits & valid(i, j))
             def _():
@@ -265,7 +262,7 @@
 
             return carry
 
-        return lax.fori_loop(0, 4, product, carry)
+        return lax.fori_loop(0, hb + 1, product, carry)
 
     lax.fori_loop(0, steps, body, 0)
 

time: 225 us -> 222 us (0.987)
  Pallas kernels: 220 us -> 215 us
    pallas_call x1, Pallas kernels: 220 us -> 215 us  [fused(): pl.pallas_call(functools.partial(fused_kernel, count), out_shape=jax.Shap...]
where the time goes in v2:
time: 222 us; the launch traced here: 220 us
  Pallas kernels  215 us (97%)
  local copies, waits for them, and re-layouts  4.7 us (2%)
    pallas_call x1, Pallas kernels, fused(): pl.pallas_call(functools.partial(fused_kernel, count), out_shape=jax.Shap...  215 us
    unnamed x1, local copies, waits for them, and re-layouts  4.7 us

profile of v2, /device:TPU:3, one launch (start us, length us, event | category | flops | bytes accessed | tf_op | source)
XLA Modules:
  0.0 220.1 jit_solution(2618561110239037723)
XLA Ops:
  0.0 215.3 %shard_map.46 = f32[512,2048]{1,0:T(8,128)} custom-call(f32[512,2048]{1,0:T(8,128)} %noise.1, f32[2048,512]{1,0:T(8,128)} %factor.1, s32[4,4]{1,0:T(4,128)} %cols.1, f32[4,4,128,128]{3,2,1,0:T(8,128)} %values.1), custom_call_target="tpu_custom_call" | custom-call | tf_op jit(solution)/shard_map/pallas_call | solution.py:296
  215.4 4.7 %copy.6 = f32[512,2048]{1,0:T(8,128)} copy(f32[512,2048]{1,0:T(8,128)} %shard_map.46) | data formatting | bytes 8388608

commit v3 on v2

--- a/solution.py
+++ b/solution.py
@@ -217,12 +217,12 @@
                 pl.when(more)(lambda: chain(i, j, way).start())
                 pl.when(apart(i) & (lax.rem(j, 2) == core))(lambda: cross(i, j).start())
 
-        before = jnp.maximum(n - 1, 0)
+        before = jnp.maximum(n - 3, 0)
         b, k = before // hb, lax.rem(before, hb)
         for way in (0, 1):
             i = source(b, way)
 
-            @pl.when((n > 0) & valid(i, k) & apart(i) & (lax.rem(k, 2) == core))
+            @pl.when((n >= 3) & valid(i, k) & apart(i) & (lax.rem(k, 2) == core))
             def _(i=i):
                 cross(i, k).wait_recv()
                 share(i, k).start()
@@ -237,21 +237,21 @@
             pl.when(m == 0)(lambda: give(c).start())
 
         for way in (0, 1):
-            i = source(a - 1, way)
-
-            @pl.when((a > 0) & valid(i, j) & ((lax.rem(j, 2) != core) | (i // 2 == d // 2)))
+            i = source(a - 2, way)
+
+            @pl.when((a > 1) & valid(i, j) & ((lax.rem(j, 2) != core) | (i // 2 == d // 2)))
             def _(i=i):
                 share(i, j).wait_recv()
 
-        early = 2 * hb - a - 1 + 0 * j
-        pl.when((j == 0) & (m == 1) & (a >= count - hb) & (a < count))(
+        early = 2 * hb - a
+        pl.when((j == 0) & (m == 1) & (a > count - hb) & (a <= count))(
             lambda: give(early).wait_recv()
         )
 
         def product(which, carry):
             i = jnp.where(which == hb, early, hb + which)
             away = jnp.maximum(jnp.maximum(d - i, i - d), count - hb)
-            fits = jnp.where(which == hb, a >= count - hb, a == away)
+            fits = jnp.where(which == hb, a > count - hb, a == away + 1)
 
             @pl.when(fits & valid(i, j))
             def _():
@@ -264,7 +264,7 @@
 
         return lax.fori_loop(0, hb + 1, product, carry)
 
-    lax.fori_loop(0, steps, body, 0)
+    lax.fori_loop(0, steps + hb, body, 0)
 
     for c in range(hb):
         halo(c, 0).wait_send()

time: 222 us -> 209 us (0.941)
  the two profiles are of different devices: /device:TPU:3 before, /device:TPU:30 now
where the time goes in v3:
time: 209 us
  Pallas kernels  205 us (98%)
  local copies, waits for them, and re-layouts  4.7 us (2%)
    pallas_call x1, Pallas kernels, fused(): pl.pallas_call(functools.partial(fused_kernel, count), out_shape=jax.Shap...  205 us
    unnamed x1, local copies, waits for them, and re-layouts  4.7 us

profile of v3, /device:TPU:30, one launch (start us, length us, event | category | flops | bytes accessed | tf_op | source)
XLA Modules:
  0.0 209.3 jit_solution(4850462481362644295)
XLA Ops:
  0.0 204.6 %shard_map.46 = f32[512,2048]{1,0:T(8,128)} custom-call(f32[512,2048]{1,0:T(8,128)} %noise.1, f32[2048,512]{1,0:T(8,128)} %factor.1, s32[4,4]{1,0:T(4,128)} %cols.1, f32[4,4,128,128]{3,2,1,0:T(8,128)} %values.1), custom_call_target="tpu_custom_call" | custom-call | tf_op jit(solution)/shard_map/pallas_call | solution.py:296
  204.6 4.7 %copy.6 = f32[512,2048]{1,0:T(8,128)} copy(f32[512,2048]{1,0:T(8,128)} %shard_map.46) | data formatting | bytes 8388608
